TPU v7x, 32 devices: a whole 2x2x4 slice. The times are simulated.
32 devices in a mesh: shard: 16 (over z, y, x), rep: 2 (over core).
Axes of the slice: x: 2, y: 2, z: 4, core: 2. Of those that a mesh axis runs over, the one named last changes fastest.
Arguments:
- tokens: bfloat16 [16384, 576], P(('shard', 'rep')), may hold values from -30 to 30
- cotangent: bfloat16 [16384, 576], P(('shard', 'rep')), may hold values from -6 to 6
- attention_gain: bfloat16 [576], P('shard'), may hold values from 0.5 to 1.5
- query_weight: bfloat16 [576, 576], P('shard'), may hold values from -0.2482166 to 0.2482166
- key_weight: bfloat16 [576, 192], P('shard'), may hold values from -0.2482166 to 0.2482166
- value_weight: bfloat16 [576, 192], P('shard'), may hold values from -0.25 to 0.25
- output_weight: bfloat16 [576, 576], P('shard'), may hold values from -1 to 1
- feedforward_gain: bfloat16 [576], P('shard'), may hold values from 0.5 to 1.5
- gate_weight: bfloat16 [576, 1536], P('shard'), may hold values from -0.25 to 0.25
- up_weight: bfloat16 [576, 1536], P('shard'), may hold values from -0.25 to 0.25
- down_weight: bfloat16 [1536, 576], P('shard'), may hold values from -0.15625 to 0.15625
Outputs:
- layer_output: bfloat16 [16384, 576], P(('shard', 'rep'))
- grad_tokens: bfloat16 [16384, 576], P(('shard', 'rep'))
- grad_attention_gain: float32 [576], P('shard')
- grad_query: float32 [576, 576], P('shard')
- grad_key: float32 [576, 192], P('shard')
- grad_value: float32 [576, 192], P('shard')
- grad_output: float32 [576, 576], P('shard')
- grad_feedforward_gain: float32 [576], P('shard')
- grad_gate: float32 [576, 1536], P('shard')
- grad_up: float32 [576, 1536], P('shard')
- grad_down: float32 [1536, 576], P('shard')
All inputs are finite; a program needn't handle non-finite values.
Results may differ from a plain program's by a relative error of at most 0.014.
The roundings to bfloat16 on the way count: a program that leaves them out, or rounds other values in their place, can miss the bound.
Values may be sent and summed in bfloat16 or wider, within the bound.
No kernel may reach another device: no remote copies, remote signals or barrier semaphores. Data moves between devices by JAX's collectives and lax.ppermute only.
A program may use at most 128 MiB of HBM per device.

v0:
```python
import jax
import jax.numpy as jnp
from jax import lax
from jax.sharding import PartitionSpec as P

H = 9
KV = 3
HD = 64


EPSILON = 1e-05


def contract_rows(former, latter):
    return lax.dot_general(
        former, latter, (((0,), (0,)), ((), ())), preferred_element_type=jnp.float32
    )


def contract_cols(former, latter):
    return lax.dot_general(
        former, latter, (((1,), (1,)), ((), ())), preferred_element_type=jnp.float32
    )


def rope_tables(length):
    half_size = HD // 2
    frequency = 10000.0 ** (-2.0 * jnp.arange(half_size, dtype=jnp.float32) / HD)
    angles = jnp.arange(length, dtype=jnp.float32)[:, None] * frequency[None, :]
    angles = jnp.concatenate([angles, angles], axis=1)
    return (jnp.cos(angles)[:, None, :], jnp.sin(angles)[:, None, :])


def rotate(values):
    half_size = values.shape[-1] // 2
    return jnp.concatenate([-values[..., half_size:], values[..., :half_size]], axis=-1)


def norm_forward(values, gain):
    scale_rows = lax.rsqrt(jnp.mean(values * values, axis=-1, keepdims=True) + EPSILON)
    normed = values * scale_rows
    return (normed, scale_rows, (normed * gain).astype(jnp.bfloat16))


def norm_backward(grad_normed_gain, normed, scale_rows, gain):
    grad_gain = jnp.sum(grad_normed_gain * normed, axis=0)
    grad_normed = grad_normed_gain * gain
    grad_input = scale_rows * (
        grad_normed - normed * jnp.mean(grad_normed * normed, axis=-1, keepdims=True)
    )
    return (grad_input, grad_gain)


def attention_scores(query_rot, key_rot, causal, scale_factor):
    raw_scores = jnp.einsum(
        "qgjd,kgd->gjqk", query_rot, key_rot, preferred_element_type=jnp.float32
    )
    return jnp.where(causal, raw_scores * scale_factor, -1e30)


def per_device(
    tokens,
    cotangent,
    attention_gain,
    query_weight,
    key_weight,
    value_weight,
    output_weight,
    feedforward_gain,
    gate_weight,
    up_weight,
    down_weight,
):
    length = tokens.shape[0]
    group_size = H // KV
    scale_factor = HD ** (-0.5)
    cos_table, sin_table = rope_tables(length)
    causal = lax.broadcasted_iota(jnp.int32, (length, length), 0) >= lax.broadcasted_iota(
        jnp.int32, (length, length), 1
    )
    attention_full = (
        lax.all_gather(attention_gain, "shard", axis=0, tiled=True),
        lax.all_gather(query_weight, "shard", axis=0, tiled=True),
        lax.all_gather(key_weight, "shard", axis=0, tiled=True),
        lax.all_gather(value_weight, "shard", axis=0, tiled=True),
        lax.all_gather(output_weight, "shard", axis=0, tiled=True),
    )
    gain_one, query_mat, key_mat, value_mat, out_mat = attention_full
    gain_one = gain_one.astype(jnp.float32)
    inputs = tokens.astype(jnp.float32)
    normed_one, scale_one, normed_low = norm_forward(inputs, gain_one)
    queries = jnp.dot(normed_low, query_mat, preferred_element_type=jnp.float32).reshape(
        length, H, HD
    )
    key_proj = jnp.dot(normed_low, key_mat, preferred_element_type=jnp.float32).reshape(
        length, KV, HD
    )
    values_low = (
        jnp.dot(normed_low, value_mat, preferred_element_type=jnp.float32)
        .astype(jnp.bfloat16)
        .reshape(length, KV, HD)
    )
    query_rot = (
        (queries * cos_table + rotate(queries) * sin_table)
        .astype(jnp.bfloat16)
        .reshape(length, KV, group_size, HD)
    )
    key_rot = (key_proj * cos_table + rotate(key_proj) * sin_table).astype(jnp.bfloat16)
    scores = attention_scores(query_rot, key_rot, causal, scale_factor)
    row_top = jnp.max(scores, axis=-1, keepdims=True)
    log_total = row_top + jnp.log(jnp.sum(jnp.exp(scores - row_top), axis=-1, keepdims=True))
    probs_low = jnp.exp(scores - log_total).astype(jnp.bfloat16)
    context_low = (
        jnp.einsum("gjqk,kgd->qgjd", probs_low, values_low, preferred_element_type=jnp.float32)
        .reshape(length, H * HD)
        .astype(jnp.bfloat16)
    )
    hidden = inputs + jnp.dot(context_low, out_mat, preferred_element_type=jnp.float32)
    feedforward_full = (
        lax.all_gather(feedforward_gain, "shard", axis=0, tiled=True),
        lax.all_gather(gate_weight, "shard", axis=0, tiled=True),
        lax.all_gather(up_weight, "shard", axis=0, tiled=True),
        lax.all_gather(down_weight, "shard", axis=0, tiled=True),
    )
    gain_two, gate_mat, up_mat, down_mat = feedforward_full
    gain_two = gain_two.astype(jnp.float32)
    normed_two, scale_two, hidden_low = norm_forward(hidden, gain_two)
    gate_pre = jnp.dot(hidden_low, gate_mat, preferred_element_type=jnp.float32)
    up_proj = jnp.dot(hidden_low, up_mat, preferred_element_type=jnp.float32)
    active_low = (jax.nn.silu(gate_pre) * up_proj).astype(jnp.bfloat16)
    layer_output = (
        hidden + jnp.dot(active_low, down_mat, preferred_element_type=jnp.float32)
    ).astype(jnp.bfloat16)
    back_gain, gate_back, up_back, down_back = (
        lax.all_gather(feedforward_gain, "shard", axis=0, tiled=True),
        lax.all_gather(gate_weight, "shard", axis=0, tiled=True),
        lax.all_gather(up_weight, "shard", axis=0, tiled=True),
        lax.all_gather(down_weight, "shard", axis=0, tiled=True),
    )
    second_back = back_gain.astype(jnp.float32)
    grad_out = cotangent.astype(jnp.float32)
    grad_down = contract_rows(active_low, cotangent)
    grad_active = contract_cols(cotangent, down_back)
    sigmoid_gate = jax.nn.sigmoid(gate_pre)
    grad_up_low = (grad_active * gate_pre * sigmoid_gate).astype(jnp.bfloat16)
    grad_gate_low = (
        grad_active * up_proj * sigmoid_gate * (1.0 + gate_pre * (1.0 - sigmoid_gate))
    ).astype(jnp.bfloat16)
    grad_gate = contract_rows(hidden_low, grad_gate_low)
    grad_up = contract_rows(hidden_low, grad_up_low)
    grad_hidden_low = contract_cols(grad_gate_low, gate_back) + contract_cols(grad_up_low, up_back)
    grad_from_two, grad_gain_two = norm_backward(
        grad_hidden_low, normed_two, scale_two, second_back
    )
    grad_hidden = grad_out + grad_from_two
    owned_gain_two, owned_gate, owned_up, owned_down = (
        lax.psum_scatter(grad_gain_two, "shard", scatter_dimension=0, tiled=True),
        lax.psum_scatter(grad_gate, "shard", scatter_dimension=0, tiled=True),
        lax.psum_scatter(grad_up, "shard", scatter_dimension=0, tiled=True),
        lax.psum_scatter(grad_down, "shard", scatter_dimension=0, tiled=True),
    )
    first_gain, query_back, key_back, value_back, out_back = (
        lax.all_gather(attention_gain, "shard", axis=0, tiled=True),
        lax.all_gather(query_weight, "shard", axis=0, tiled=True),
        lax.all_gather(key_weight, "shard", axis=0, tiled=True),
        lax.all_gather(value_weight, "shard", axis=0, tiled=True),
        lax.all_gather(output_weight, "shard", axis=0, tiled=True),
    )
    first_back = first_gain.astype(jnp.float32)
    grad_attn_low = grad_hidden.astype(jnp.bfloat16)
    grad_output = contract_rows(context_low, grad_attn_low)
    grad_context_low = (
        contract_cols(grad_attn_low, out_back)
        .astype(jnp.bfloat16)
        .reshape(length, KV, group_size, HD)
    )
    scores_again = attention_scores(query_rot, key_rot, causal, scale_factor)
    probability = jnp.exp(scores_again - log_total)
    probs_again = probability.astype(jnp.bfloat16)
    grad_probs = jnp.einsum(
        "qgjd,kgd->gjqk", grad_context_low, values_low, preferred_element_type=jnp.float32
    )
    grad_values_low = (
        jnp.einsum(
            "gjqk,qgjd->kgd", probs_again, grad_context_low, preferred_element_type=jnp.float32
        )
        .astype(jnp.bfloat16)
        .reshape(length, KV * HD)
    )
    grad_scores = probability * (
        grad_probs - jnp.sum(probability * grad_probs, axis=-1, keepdims=True)
    )
    grad_scores_low = grad_scores.astype(jnp.bfloat16)
    grad_query_rot = (
        jnp.einsum("gjqk,kgd->qgjd", grad_scores_low, key_rot, preferred_element_type=jnp.float32)
        * scale_factor
    ).reshape(length, H, HD)
    grad_key_rot = (
        jnp.einsum("gjqk,qgjd->kgd", grad_scores_low, query_rot, preferred_element_type=jnp.float32)
        * scale_factor
    )
    grad_query_low = (
        (grad_query_rot * cos_table - rotate(grad_query_rot * sin_table))
        .astype(jnp.bfloat16)
        .reshape(length, H * HD)
    )
    grad_key_low = (
        (grad_key_rot * cos_table - rotate(grad_key_rot * sin_table))
        .astype(jnp.bfloat16)
        .reshape(length, KV * HD)
    )
    grad_query = contract_rows(normed_low, grad_query_low)
    grad_key = contract_rows(normed_low, grad_key_low)
    grad_value = contract_rows(normed_low, grad_values_low)
    grad_normed_low = (
        contract_cols(grad_query_low, query_back)
        + contract_cols(grad_key_low, key_back)
        + contract_cols(grad_values_low, value_back)
    )
    grad_from_one, grad_gain_one = norm_backward(grad_normed_low, normed_one, scale_one, first_back)
    grad_tokens = (grad_hidden + grad_from_one).astype(jnp.bfloat16)
    owned_gain_one, owned_query, owned_key, owned_value, owned_output = (
        lax.psum_scatter(grad_gain_one, "shard", scatter_dimension=0, tiled=True),
        lax.psum_scatter(grad_query, "shard", scatter_dimension=0, tiled=True),
        lax.psum_scatter(grad_key, "shard", scatter_dimension=0, tiled=True),
        lax.psum_scatter(grad_value, "shard", scatter_dimension=0, tiled=True),
        lax.psum_scatter(grad_output, "shard", scatter_dimension=0, tiled=True),
    )
    totals = lax.psum(
        (
            owned_gain_one,
            owned_query,
            owned_key,
            owned_value,
            owned_output,
            owned_gain_two,
            owned_gate,
            owned_up,
            owned_down,
        ),
        "rep",
    )
    owned_gain_one, owned_query, owned_key, owned_value, owned_output = (
        totals[0],
        totals[1],
        totals[2],
        totals[3],
        totals[4],
    )
    owned_gain_two, owned_gate, owned_up, owned_down = (totals[5], totals[6], totals[7], totals[8])
    return (
        layer_output,
        grad_tokens,
        owned_gain_one,
        owned_query,
        owned_key,
        owned_value,
        owned_output,
        owned_gain_two,
        owned_gate,
        owned_up,
        owned_down,
    )


def solution(mesh):
    placed = (
        P(("shard", "rep"), None),
        P(("shard", "rep"), None),
        P("shard"),
        P("shard", None),
        P("shard", None),
        P("shard", None),
        P("shard", None),
        P("shard"),
        P("shard", None),
        P("shard", None),
        P("shard", None),
    )
    return jax.shard_map(
        per_device,
        mesh=mesh,
        in_specs=placed,
        out_specs=(
            P(("shard", "rep"), None),
            P(("shard", "rep"), None),
            P("shard"),
            P("shard", None),
            P("shard", None),
            P("shard", None),
            P("shard", None),
            P("shard"),
            P("shard", None),
            P("shard", None),
            P("shard", None),
        ),
        check_vma=False,
    )
```

profile of v0, /device:TPU:0, one launch (start us, length us, event | category | flops | bytes accessed | tf_op | source)
XLA Modules:
  0.0 714.9 jit_solution(9957177394852842875)
XLA Ops:
  9.6 45.0 %all-gather = bf16[16,36,192]{2,1,0:T(8,128)(2,1)S(1)} all-gather(bf16[1,36,192]{2,1,0:T(8,128)(2,1)} %bitcast.159), channel_id=1, replica_groups=mesh['shard'=16,'rep'=2] {'shard'}, dimensions={0}, use_global_device_ids=true | all-gather | bytes 235008 | tf_op jit(solution)/shard_map/all_gather | solution.py:85
  57.2 36.8 %all-reduce.19 = (bf16[576]{0:T(1024)(128)(2,1)S(1)}, bf16[576]{0:T(1024)(128)(2,1)S(1)}) all-reduce(bf16[576]{0:T(1024)(128)(2,1)S(1)} %dynamic-update-slice, bf16[576]{0:T(1024)(128)(2,1)S(1)} %dynamic-update-slice.1), channel_id=1, replica_groups=mesh['shard'=16,'rep'=2] {'shard'}, use_global_device_ids=true, to_apply=%add | all-reduce | flops 1152 | bytes 4608
  94.1 40.4 %all-gather.1 = bf16[16,36,192]{2,1,0:T(8,128)(2,1)S(1)} all-gather(bf16[1,36,192]{2,1,0:T(8,128)(2,1)S(1)} %bitcast.160), channel_id=1, replica_groups=mesh['shard'=16,'rep'=2] {'shard'}, dimensions={0}, use_global_device_ids=true | all-gather | bytes 235008 | tf_op jit(solution)/shard_map/all_gather | solution.py:84
  137.1 43.8 %all-gather.2 = bf16[16,36,576]{2,1,0:T(8,128)(2,1)S(1)} all-gather(bf16[1,36,576]{2,1,0:T(8,128)(2,1)S(1)} %bitcast.157), channel_id=1, replica_groups=mesh['shard'=16,'rep'=2] {'shard'}, dimensions={0}, use_global_device_ids=true | all-gather | bytes 705024 | tf_op jit(solution)/shard_map/all_gather | solution.py:83
  183.0 42.5 %all-gather.3 = bf16[16,36,576]{2,1,0:T(8,128)(2,1)S(1)} all-gather(bf16[1,36,576]{2,1,0:T(8,128)(2,1)S(1)} %bitcast.158), channel_id=1, replica_groups=mesh['shard'=16,'rep'=2] {'shard'}, dimensions={0}, use_global_device_ids=true | all-gather | bytes 705024 | tf_op jit(solution)/shard_map/all_gather | solution.py:86
  240.2 3.7 reshape.159
  243.9 3.5 reshape.161
  247.4 4.8 fusion.53
  252.2 3.0 fusion.54
  255.2 5.2 multiply_convert_fusion
  267.3 5.5 fusion.6
  272.8 3.4 fusion.58
  276.5 11.4 %fusion.8 = bf16[3,3,512,512]{2,3,1,0:T(8,128)(2,1)} fusion(f32[3,512,512,3]{2,1,3,0:T(8,128)} %get-tuple-element.64, f32[3,512,512,3]{2,1,3,0:T(8,128)} %copy-done, f32[3,3,512]{2,1,0:T(4,128)S(1)} %get-tuple-element.63, f32[3,3,512]{2,1,0:T(4,128)S(1)} %log_add_fusion, pred[512,512]{0,1:T(8,128)(4,1)S(1)} %iota_compare_fusion), kind=kLoop, calls=%fused_computation.4 | loop fusion | flops 14155776 | bytes 23891968 | tf_op jit(solution)/shard_map/convert_element_type | solution.py:193
  288.0 3.3 convolution_multiply_fusion
  305.5 2.8 fusion.56
  308.3 2.8 fusion.57
  311.2 251.8 %fusion.51 = (f32[40,192]{1,0:T(8,128)}, f32[40,192]{1,0:T(8,128)S(1)}, f32[48,576]{1,0:T(8,128)}, f32[48,576]{1,0:T(8,128)}, f32[40,1536]{1,0:T(8,128)S(1)}, /*index=5*/f32[40,1536]{1,0:T(8,128)S(1)}) fusion(f32[576,192]{1,0:T(8,128)} %fusion.42, f32[576,192]{1,0:T(8,128)} %fusion.40, f32[576,576]{1,0:T(8,128)} %fusion.44, f32[576,576]{1,0:T(8,128)} %fusion.32, ...), kind=kCustom, calls=%all-reduce-scatter.6 | all-reduce-scatter fusion | flops 3096578 | bytes 11391488
  563.9 6.6 collective-permute-start.2
  571.7 3.1 collective-permute-start
  576.4 4.0 fusion.15
  582.6 6.5 collective-permute-start.10
  589.1 4.0 collective-permute-start.9
  595.0 2.5 collective-permute-start.12
  597.6 2.9 collective-permute-start.14
  604.1 7.9 %concatenate.38 = f32[228,576]{1,0:T(8,128)} concatenate(f32[36,576]{1,0:T(8,128)} %copy-done.47, f32[48,576]{1,0:T(8,128)} %copy-done.44, f32[48,576]{1,0:T(8,128)} %copy-done.45, f32[48,576]{1,0:T(8,128)} %copy-done.46, f32[48,576]{1,0:T(8,128)} %get-tuple-element.36), dimensions={0} | concatenate | bytes 1050624
  620.7 3.4 collective-permute-start.4
  624.1 7.9 %concatenate.41 = f32[228,576]{1,0:T(8,128)} concatenate(f32[36,576]{1,0:T(8,128)} %collective-permute-done.11, f32[48,576]{1,0:T(8,128)} %collective-permute-done.10, f32[48,576]{1,0:T(8,128)} %collective-permute-done.9, f32[48,576]{1,0:T(8,128)} %collective-permute-done.8, f32[48,576]{1,0:T(8,128)} %get-tuple-element.37), dimensions={0} | concatenate | bytes 1050624
  635.5 2.8 collective-permute-start.5
  638.3 4.9 concatenate.42
  645.2 4.9 concatenate.43
  655.2 37.1 %all-reduce.16 = (f32[576]{0:T(1024)S(1)}, f32[576]{0:T(1024)S(1)}) all-reduce(f32[576]{0:T(1024)S(1)} %get-tuple-element.13, f32[576]{0:T(1024)S(1)} %copy-done.52), channel_id=2, replica_groups=mesh['shard'=16,'rep'=2] {'shard'}, use_global_device_ids=true, to_apply=%region_8.9.clone | all-reduce | flops 1152 | bytes 9216
  696.6 4.2 all-reduce.17
  (237 shorter events, 84.9 us)
Async XLA Ops:
  7.2 48.2 %copy-start.51 = (u32[32]{0:T(128)S(1)}, u32[32]{0:T(128)}, u32[]{:S(2)}) copy-start(u32[32]{0:T(128)} %constant.39) | copy-start | bytes 388
  7.2 49.5 %copy-start.53 = (bf16[36]{0:T(256)(128)(2,1)S(1)}, bf16[36]{0:T(256)(128)(2,1)}, u32[]{:S(2)}) copy-start(bf16[36]{0:T(256)(128)(2,1)} %param.13) | copy-start | bytes 220
  7.2 49.7 %copy-start.54 = (bf16[36]{0:T(256)(128)(2,1)S(1)}, bf16[36]{0:T(256)(128)(2,1)}, u32[]{:S(2)}) copy-start(bf16[36]{0:T(256)(128)(2,1)} %param.18) | copy-start | bytes 220
  7.2 86.8 %copy-start.2 = (bf16[512,576]{0,1:T(8,128)(2,1)S(1)}, bf16[512,576]{0,1:T(8,128)(2,1)}, u32[]{:S(2)}) copy-start(bf16[512,576]{0,1:T(8,128)(2,1)} %param.11) | copy-start | bytes 1769476
  7.2 86.9 %copy-start.50 = (bf16[36,192]{1,0:T(8,128)(2,1)S(1)}, bf16[36,192]{1,0:T(8,128)(2,1)}, u32[]{:S(2)}) copy-start(bf16[36,192]{1,0:T(8,128)(2,1)} %param.15) | copy-start | bytes 41476
  7.2 232.9 %all-gather.12.cloned.1.call-start = ((), (), s32[]{:S(2)}) async-start(), calls=%async_computation.3 | async-start | bytes 2088960 | tf_op jit(solution)/shard_map/all_gather | solution.py:121
  8.0 235.9 %all-gather.14.cloned.1.call-start = ((), (), s32[]{:S(2)}) async-start(), calls=%async_computation.4 | async-start | bytes 2088960 | tf_op jit(solution)/shard_map/all_gather | solution.py:122
  8.7 246.5 %all-gather.10.cloned.1.call-start = ((), (), s32[]{:S(2)}) async-start(), calls=%async_computation.1 | async-start | bytes 2088960 | tf_op jit(solution)/shard_map/all_gather | solution.py:123
  9.4 644.0 %reduce-scatter.14.cloned.1.call-start = ((), (), s32[]{:S(2)}) async-start(), calls=%async_computation.2 | async-start | bytes 4177920 | tf_op jit(solution)/shard_map/reduce_scatter | solution.py:160
  260.5 12.3 %copy-start.13 = (bf16[512,1536]{1,0:T(8,128)(2,1)}, bf16[512,1536]{1,0:T(8,128)(2,1)S(1)}, u32[]{:S(2)}) copy-start(bf16[512,1536]{1,0:T(8,128)(2,1)S(1)} %get-tuple-element.42) | copy-start | bytes 4718596
  276.3 424.5 %all-reduce.23.cloned.1.call-start = ((), (), s32[]{:S(2)}) async-start(), calls=%async_computation.5 | async-start | bytes 1884160 | tf_op jit(solution)/shard_map/psum | solution.py:229
  563.8 16.5 %copy-start.6 = (bf16[576,576]{1,0:T(8,128)(2,1)S(1)}, bf16[576,576]{1,0:T(8,128)(2,1)}, u32[]{:S(2)}) copy-start(bf16[576,576]{1,0:T(8,128)(2,1)} %copy-done.5) | copy-start | bytes 1990660
  563.9 16.5 %copy-start.12 = (bf16[512,576]{0,1:T(8,128)(2,1)S(1)}, bf16[512,576]{0,1:T(8,128)(2,1)}, u32[]{:S(2)}) copy-start(bf16[512,576]{0,1:T(8,128)(2,1)} %copy-done.11) | copy-start | bytes 1769476
  563.9 29.2 %collective-permute-start.2 = (f32[48,576]{1,0:T(8,128)}, f32[48,576]{1,0:T(8,128)S(1)}, u32[]{:S(2)}, u32[]{:S(2)}) collective-permute-start(f32[48,576]{1,0:T(8,128)} %get-tuple-element.36), channel_id=1, source_target_pairs={{0,6},{2,8},{4,10},{6,12},{8,14},{10,16},{12,18},{14,20},{16,22},{... | collective-permute-start | bytes 331784
  570.4 24.6 %collective-permute-start.1 = (f32[48,576]{1,0:T(8,128)}, f32[48,576]{1,0:T(8,128)S(1)}, u32[]{:S(2)}, u32[]{:S(2)}) collective-permute-start(f32[48,576]{1,0:T(8,128)} %get-tuple-element.36), channel_id=1, source_target_pairs={{0,4},{2,6},{4,8},{6,10},{8,12},{10,14},{12,16},{14,18},{16,20},{1... | collective-permute-start | bytes 331784
  571.7 25.8 %collective-permute-start = (f32[48,576]{1,0:T(8,128)}, f32[48,576]{1,0:T(8,128)S(1)}, u32[]{:S(2)}, u32[]{:S(2)}) collective-permute-start(f32[48,576]{1,0:T(8,128)} %get-tuple-element.36), channel_id=1, source_target_pairs={{0,2},{2,4},{4,6},{6,8},{8,10},{10,12},{12,14},{14,16},{16,18},{18... | collective-permute-start | bytes 331784
  574.8 14.3 %collective-permute-start.3 = (f32[36,576]{1,0:T(8,128)S(1)}, f32[36,576]{1,0:T(8,128)S(1)}, u32[]{:S(2)}, u32[]{:S(2)}) collective-permute-start(f32[36,576]{1,0:T(8,128)S(1)} %slice.40), channel_id=1, source_target_pairs={{0,8},{2,10},{4,12},{6,14},{8,16},{10,18},{12,20},{14,22},{16,24},... | collective-permute-start | bytes 248840
  580.4 20.1 %copy-start.37 = (bf16[576,192]{1,0:T(8,128)(2,1)S(1)}, bf16[576,192]{1,0:T(8,128)(2,1)}, u32[]{:S(2)}) copy-start(bf16[576,192]{1,0:T(8,128)(2,1)} %copy-done.36) | copy-start | bytes 663556
  580.4 20.1 %copy-start.39 = (bf16[512,3,64]{0,2,1:T(8,128)(2,1)S(1)}, bf16[512,3,64]{0,2,1:T(8,128)(2,1)}, u32[]{:S(2)}) copy-start(bf16[512,3,64]{0,2,1:T(8,128)(2,1)} %copy-done.38) | copy-start | bytes 589828
  582.6 31.9 %collective-permute-start.10 = (f32[48,576]{1,0:T(8,128)}, f32[48,576]{1,0:T(8,128)}, u32[]{:S(2)}, u32[]{:S(2)}) collective-permute-start(f32[48,576]{1,0:T(8,128)} %get-tuple-element.37), channel_id=1, source_target_pairs={{0,6},{2,8},{4,10},{6,12},{8,14},{10,16},{12,18},{14,20},{16,22},{... | collective-permute-start | bytes 331784
  589.1 12.3 %copy-start.47 = (f32[36,576]{1,0:T(8,128)}, f32[36,576]{1,0:T(8,128)S(1)}, u32[]{:S(2)}) copy-start(f32[36,576]{1,0:T(8,128)S(1)} %collective-permute-done.3) | copy-start | bytes 248836
  589.1 27.5 %collective-permute-start.9 = (f32[48,576]{1,0:T(8,128)}, f32[48,576]{1,0:T(8,128)}, u32[]{:S(2)}, u32[]{:S(2)}) collective-permute-start(f32[48,576]{1,0:T(8,128)} %get-tuple-element.37), channel_id=1, source_target_pairs={{0,4},{2,6},{4,8},{6,10},{8,12},{10,14},{12,16},{14,18},{16,20},{1... | collective-permute-start | bytes 331784
  593.1 18.8 %collective-permute-start.11 = (f32[36,576]{1,0:T(8,128)}, f32[36,576]{1,0:T(8,128)}, u32[]{:S(2)}, u32[]{:S(2)}) collective-permute-start(f32[36,576]{1,0:T(8,128)} %slice.43), channel_id=1, source_target_pairs={{0,8},{2,10},{4,12},{6,14},{8,16},{10,18},{12,20},{14,22},{16,24},... | collective-permute-start | bytes 248840
  595.0 40.5 %collective-permute-start.12 = (f32[40,1536]{1,0:T(8,128)S(1)}, f32[40,1536]{1,0:T(8,128)}, u32[]{:S(2)}, u32[]{:S(2)}) collective-permute-start(f32[40,1536]{1,0:T(8,128)S(1)} %get-tuple-element.38), channel_id=1, source_target_pairs={{0,2},{2,4},{4,6},{6,8},{8,10},{10,12},{12,14},{14,16},{16,18},{18... | collective-permute-start | bytes 737288
  597.6 47.6 %collective-permute-start.14 = (f32[40,1536]{1,0:T(8,128)S(1)}, f32[40,1536]{1,0:T(8,128)}, u32[]{:S(2)}, u32[]{:S(2)}) collective-permute-start(f32[40,1536]{1,0:T(8,128)S(1)} %get-tuple-element.39), channel_id=1, source_target_pairs={{0,2},{2,4},{4,6},{6,8},{8,10},{10,12},{12,14},{14,16},{16,18},{18... | collective-permute-start | bytes 737288
  612.0 8.7 %collective-permute-start.8 = (f32[48,576]{1,0:T(8,128)}, f32[48,576]{1,0:T(8,128)}, u32[]{:S(2)}, u32[]{:S(2)}) collective-permute-start(f32[48,576]{1,0:T(8,128)} %get-tuple-element.37), channel_id=1, source_target_pairs={{0,2},{2,4},{4,6},{6,8},{8,10},{10,12},{12,14},{14,16},{16,18},{18... | collective-permute-start | bytes 331784
  614.4 19.1 %collective-permute-start.13 = (f32[20,1536]{1,0:T(8,128)}, f32[20,1536]{1,0:T(8,128)}, u32[]{:S(2)}, u32[]{:S(2)}) collective-permute-start(f32[20,1536]{1,0:T(8,128)} %slice.44), channel_id=1, source_target_pairs={{0,4},{2,6},{4,8},{6,10},{8,12},{10,14},{12,16},{14,18},{16,20},{1... | collective-permute-start | bytes 368648
  616.6 26.5 %collective-permute-start.15 = (f32[20,1536]{1,0:T(8,128)}, f32[20,1536]{1,0:T(8,128)}, u32[]{:S(2)}, u32[]{:S(2)}) collective-permute-start(f32[20,1536]{1,0:T(8,128)} %slice.45), channel_id=1, source_target_pairs={{0,4},{2,6},{4,8},{6,10},{8,12},{10,14},{12,16},{14,18},{16,20},{1... | collective-permute-start | bytes 368648
  620.7 71.8 %collective-permute-start.4 = (f32[40,192]{1,0:T(8,128)}, f32[40,192]{1,0:T(8,128)}, u32[]{:S(2)}, u32[]{:S(2)}) collective-permute-start(f32[40,192]{1,0:T(8,128)} %get-tuple-element.34), channel_id=1, source_target_pairs={{0,2},{2,4},{4,6},{6,8},{8,10},{10,12},{12,14},{14,16},{16,18},{18... | collective-permute-start | bytes 92168
  633.6 61.3 %collective-permute-start.6 = (f32[40,192]{1,0:T(8,128)S(1)}, f32[40,192]{1,0:T(8,128)}, u32[]{:S(2)}, u32[]{:S(2)}) collective-permute-start(f32[40,192]{1,0:T(8,128)S(1)} %get-tuple-element.35), channel_id=1, source_target_pairs={{0,2},{2,4},{4,6},{6,8},{8,10},{10,12},{12,14},{14,16},{16,18},{18... | collective-permute-start | bytes 92168
  635.5 57.0 %collective-permute-start.5 = (f32[20,192]{1,0:T(8,128)}, f32[20,192]{1,0:T(8,128)}, u32[]{:S(2)}, u32[]{:S(2)}) collective-permute-start(f32[20,192]{1,0:T(8,128)} %slice.41), channel_id=1, source_target_pairs={{0,4},{2,6},{4,8},{6,10},{8,12},{10,14},{12,16},{14,18},{16,20},{1... | collective-permute-start | bytes 46088
  643.1 51.7 %collective-permute-start.7 = (f32[20,192]{1,0:T(8,128)}, f32[20,192]{1,0:T(8,128)}, u32[]{:S(2)}, u32[]{:S(2)}) collective-permute-start(f32[20,192]{1,0:T(8,128)} %slice.42), channel_id=1, source_target_pairs={{0,4},{2,6},{4,8},{6,10},{8,12},{10,14},{12,16},{14,18},{16,20},{1... | collective-permute-start | bytes 46088
  (50 other events, 201.9 us)
Sparse Core Ops, SparseCore 0:
  10.9 62.9 all-gather.11
  76.7 61.2 all-gather.13
  140.8 63.3 all-gather.9
  276.4 167.4 reduce-scatter.13
  653.6 15.4 all-reduce.22
where the time goes:
time: 725 us; the launch traced here: 715 us
  blocking collectives  502 us (69%)
  local copies, waits for them, and re-layouts  67.3 us (9%)
  matrix products  56.4 us (8%)
  starting transfers between devices  48.1 us (7%)
  other arithmetic  21.7 us (3%)
  between operations  17.7 us (2%)
    unnamed x3, blocking collectives  326 us
    unnamed x158, local copies, waits for them, and re-layouts  67.3 us
    unnamed x16, starting transfers between devices  47.7 us
    all_gather x1, blocking collectives, per_device(): lax.all_gather(value_weight, 'shard', axis=0, tiled=True)  45 us
    all_gather x1, blocking collectives, per_device(): lax.all_gather(query_weight, 'shard', axis=0, tiled=True)  43.8 us
    all_gather x1, blocking collectives, per_device(): lax.all_gather(output_weight, 'shard', axis=0, tiled=True)  42.5 us
    all_gather x1, blocking collectives, per_device(): lax.all_gather(key_weight, 'shard', axis=0, tiled=True)  40.4 us
    dot_general x7, matrix products, contract_rows(): lax.dot_general(former, latter, (((0,), (0,)), ((), ())), preferred_eleme...  15.1 us
  transfers between devices with their start and end apart: 21, of which 0 were waited for; matrix products, arithmetic and copies ran while one was open for 51% of the time, Pallas kernels for 0%

commit v1 on v0

v1 whole, which is shorter than its diff:
```python
import jax
import jax.numpy as jnp
from jax import lax
from jax.sharding import PartitionSpec as P

H = 9
KV = 3
HD = 64


EPSILON = 1e-05


def contract_rows(former, latter):
    return lax.dot_general(
        former, latter, (((0,), (0,)), ((), ())), preferred_element_type=jnp.float32
    )


def contract_cols(former, latter):
    return lax.dot_general(
        former, latter, (((1,), (1,)), ((), ())), preferred_element_type=jnp.float32
    )


def rope_tables(length):
    half_size = HD // 2
    frequency = 10000.0 ** (-2.0 * jnp.arange(half_size, dtype=jnp.float32) / HD)
    angles = jnp.arange(length, dtype=jnp.float32)[:, None] * frequency[None, :]
    angles = jnp.concatenate([angles, angles], axis=1)
    return (jnp.cos(angles)[:, None, :], jnp.sin(angles)[:, None, :])


def rotate(values):
    half_size = values.shape[-1] // 2
    return jnp.concatenate([-values[..., half_size:], values[..., :half_size]], axis=-1)


def norm_forward(values, gain):
    scale_rows = lax.rsqrt(jnp.mean(values * values, axis=-1, keepdims=True) + EPSILON)
    normed = values * scale_rows
    return (normed, scale_rows, (normed * gain).astype(jnp.bfloat16))


def norm_backward(grad_normed_gain, normed, scale_rows, gain):
    grad_gain = jnp.sum(grad_normed_gain * normed, axis=0)
    grad_normed = grad_normed_gain * gain
    grad_input = scale_rows * (
        grad_normed - normed * jnp.mean(grad_normed * normed, axis=-1, keepdims=True)
    )
    return (grad_input, grad_gain)


def attention_scores(query_rot, key_rot, causal, scale_factor):
    raw_scores = jnp.einsum(
        "qgjd,kgd->gjqk", query_rot, key_rot, preferred_element_type=jnp.float32
    )
    return jnp.where(causal, raw_scores * scale_factor, -1e30)


def phases_of(n):
    out, stride = [], 1
    while stride < n:
        size = 4 if n // stride % 4 == 0 else 2
        out.append((stride, size))
        stride *= size
    return out


def groups_of(n, stride, size):
    return [
        [base + stride * j for j in range(size)]
        for base in range(n)
        if base // stride % size == 0
    ]


def swap_cores(value):
    return lax.ppermute(value, "rep", [(0, 1), (1, 0)])


def gather_half(n, block):
    rows, cols = block.shape
    held = block[None]
    dims = []
    for stride, size in reversed(phases_of(n)):
        sent = jnp.broadcast_to(held[None], (size,) + held.shape)
        held = lax.all_to_all(
            sent, "shard", 0, 0, tiled=True, axis_index_groups=groups_of(n, stride, size)
        )
        held = held.reshape((-1, rows, cols))
        dims.append(size)
    held = held.reshape(tuple(reversed(dims)) + (rows, cols))
    order = tuple(reversed(range(len(dims)))) + (len(dims), len(dims) + 1)
    return held.transpose(order).reshape((n, rows, cols))


def gather_pair(n, first, second):
    core = lax.axis_index("rep")
    mine = gather_half(n, jnp.where(core == 0, first, second))
    other = swap_cores(mine)
    return jnp.where(core == 0, mine, other), jnp.where(core == 0, other, mine)


def scatter_pair(n, first, second):
    core = lax.axis_index("rep")
    first, second = first.astype(jnp.bfloat16), second.astype(jnp.bfloat16)
    keep = jnp.where(core == 0, first, second)
    send = jnp.where(core == 0, second, first)
    held = keep.astype(jnp.float32) + swap_cores(send).astype(jnp.float32)
    rows, cols = held.shape[1:]
    sizes = [size for _, size in phases_of(n)]
    for stride, size in phases_of(n):
        held = held.astype(jnp.bfloat16)
        left = held.shape[0] // size
        sent = held.reshape((left, size, rows, cols)).swapaxes(0, 1)
        got = lax.all_to_all(
            sent, "shard", 0, 0, tiled=True, axis_index_groups=groups_of(n, stride, size)
        )
        held = jnp.sum(got.astype(jnp.float32), axis=0)
    mine = held[0]
    other = swap_cores(mine)
    return jnp.where(core == 0, mine, other), jnp.where(core == 0, other, mine)


def per_device(
    n,
    tokens,
    cotangent,
    attention_gain,
    query_weight,
    key_weight,
    value_weight,
    output_weight,
    feedforward_gain,
    gate_weight,
    up_weight,
    down_weight,
):
    length, width = tokens.shape
    group_size = H // KV
    scale_factor = HD ** (-0.5)
    own_rows = width // n
    q_cols, kv_cols = H * HD, KV * HD
    cos_table, sin_table = rope_tables(length)
    causal = lax.broadcasted_iota(jnp.int32, (length, length), 0) >= lax.broadcasted_iota(
        jnp.int32, (length, length), 1
    )

    def with_gain(weights, gain):
        row = jnp.pad(gain, (0, weights.shape[1] - gain.shape[0]))
        return jnp.concatenate([weights, row[None]], axis=0)

    first, second = gather_pair(
        n,
        with_gain(jnp.concatenate([query_weight, key_weight], axis=1), attention_gain),
        with_gain(jnp.concatenate([value_weight, output_weight], axis=1), feedforward_gain),
    )
    query_mat = first[:, :own_rows, :q_cols].reshape((width, q_cols))
    key_mat = first[:, :own_rows, q_cols:].reshape((width, kv_cols))
    value_mat = second[:, :own_rows, :kv_cols].reshape((width, kv_cols))
    out_mat = second[:, :own_rows, kv_cols:].reshape((q_cols, width))
    gain_one = first[:, own_rows, :own_rows].reshape((width,)).astype(jnp.float32)
    gain_two = second[:, own_rows, :own_rows].reshape((width,)).astype(jnp.float32)

    gate_mat, up_mat = gather_pair(n, gate_weight, up_weight)
    gate_mat = gate_mat.reshape((width, -1))
    up_mat = up_mat.reshape((width, -1))
    down_rows = down_weight.shape[0]
    down_first, down_second = gather_pair(
        n, down_weight[: down_rows // 2], down_weight[down_rows // 2 :]
    )
    down_mat = jnp.concatenate([down_first, down_second], axis=1).reshape((-1, width))

    inputs = tokens.astype(jnp.float32)
    normed_one, scale_one, normed_low = norm_forward(inputs, gain_one)
    queries = jnp.dot(normed_low, query_mat, preferred_element_type=jnp.float32).reshape(
        length, H, HD
    )
    key_proj = jnp.dot(normed_low, key_mat, preferred_element_type=jnp.float32).reshape(
        length, KV, HD
    )
    values_low = (
        jnp.dot(normed_low, value_mat, preferred_element_type=jnp.float32)
        .astype(jnp.bfloat16)
        .reshape(length, KV, HD)
    )
    query_rot = (
        (queries * cos_table + rotate(queries) * sin_table)
        .astype(jnp.bfloat16)
        .reshape(length, KV, group_size, HD)
    )
    key_rot = (key_proj * cos_table + rotate(key_proj) * sin_table).astype(jnp.bfloat16)
    scores = attention_scores(query_rot, key_rot, causal, scale_factor)
    row_top = jnp.max(scores, axis=-1, keepdims=True)
    log_total = row_top + jnp.log(jnp.sum(jnp.exp(scores - row_top), axis=-1, keepdims=True))
    probs_low = jnp.exp(scores - log_total).astype(jnp.bfloat16)
    context_low = (
        jnp.einsum("gjqk,kgd->qgjd", probs_low, values_low, preferred_element_type=jnp.float32)
        .reshape(length, H * HD)
        .astype(jnp.bfloat16)
    )
    hidden = inputs + jnp.dot(context_low, out_mat, preferred_element_type=jnp.float32)
    normed_two, scale_two, hidden_low = norm_forward(hidden, gain_two)
    gate_pre = jnp.dot(hidden_low, gate_mat, preferred_element_type=jnp.float32)
    up_proj = jnp.dot(hidden_low, up_mat, preferred_element_type=jnp.float32)
    active_low = (jax.nn.silu(gate_pre) * up_proj).astype(jnp.bfloat16)
    layer_output = (
        hidden + jnp.dot(active_low, down_mat, preferred_element_type=jnp.float32)
    ).astype(jnp.bfloat16)
    grad_out = cotangent.astype(jnp.float32)
    grad_down = contract_rows(active_low, cotangent).reshape((n, 2, down_rows // 2, width))
    owned_down = jnp.concatenate(scatter_pair(n, grad_down[:, 0], grad_down[:, 1]), axis=0)
    grad_active = contract_cols(cotangent, down_mat)
    sigmoid_gate = jax.nn.sigmoid(gate_pre)
    grad_up_low = (grad_active * gate_pre * sigmoid_gate).astype(jnp.bfloat16)
    grad_gate_low = (
        grad_active * up_proj * sigmoid_gate * (1.0 + gate_pre * (1.0 - sigmoid_gate))
    ).astype(jnp.bfloat16)
    grad_gate = contract_rows(hidden_low, grad_gate_low)
    grad_up = contract_rows(hidden_low, grad_up_low)
    owned_gate, owned_up = scatter_pair(
        n, grad_gate.reshape((n, own_rows, -1)), grad_up.reshape((n, own_rows, -1))
    )
    grad_hidden_low = contract_cols(grad_gate_low, gate_mat) + contract_cols(grad_up_low, up_mat)
    grad_from_two, grad_gain_two = norm_backward(grad_hidden_low, normed_two, scale_two, gain_two)
    grad_hidden = grad_out + grad_from_two
    grad_attn_low = grad_hidden.astype(jnp.bfloat16)
    grad_output = contract_rows(context_low, grad_attn_low)
    grad_context_low = (
        contract_cols(grad_attn_low, out_mat)
        .astype(jnp.bfloat16)
        .reshape(length, KV, group_size, HD)
    )
    scores_again = attention_scores(query_rot, key_rot, causal, scale_factor)
    probability = jnp.exp(scores_again - log_total)
    probs_again = probability.astype(jnp.bfloat16)
    grad_probs = jnp.einsum(
        "qgjd,kgd->gjqk", grad_context_low, values_low, preferred_element_type=jnp.float32
    )
    grad_values_low = (
        jnp.einsum(
            "gjqk,qgjd->kgd", probs_again, grad_context_low, preferred_element_type=jnp.float32
        )
        .astype(jnp.bfloat16)
        .reshape(length, KV * HD)
    )
    grad_scores = probability * (
        grad_probs - jnp.sum(probability * grad_probs, axis=-1, keepdims=True)
    )
    grad_scores_low = grad_scores.astype(jnp.bfloat16)
    grad_query_rot = (
        jnp.einsum("gjqk,kgd->qgjd", grad_scores_low, key_rot, preferred_element_type=jnp.float32)
        * scale_factor
    ).reshape(length, H, HD)
    grad_key_rot = (
        jnp.einsum("gjqk,qgjd->kgd", grad_scores_low, query_rot, preferred_element_type=jnp.float32)
        * scale_factor
    )
    grad_query_low = (
        (grad_query_rot * cos_table - rotate(grad_query_rot * sin_table))
        .astype(jnp.bfloat16)
        .reshape(length, H * HD)
    )
    grad_key_low = (
        (grad_key_rot * cos_table - rotate(grad_key_rot * sin_table))
        .astype(jnp.bfloat16)
        .reshape(length, KV * HD)
    )
    grad_query = contract_rows(normed_low, grad_query_low)
    grad_key = contract_rows(normed_low, grad_key_low)
    grad_value = contract_rows(normed_low, grad_values_low)
    grad_normed_low = (
        contract_cols(grad_query_low, query_mat)
        + contract_cols(grad_key_low, key_mat)
        + contract_cols(grad_values_low, value_mat)
    )
    grad_from_one, grad_gain_one = norm_backward(grad_normed_low, normed_one, scale_one, gain_one)
    grad_tokens = (grad_hidden + grad_from_one).astype(jnp.bfloat16)

    def grads_with_gain(left, right, gain):
        both = jnp.concatenate([left, right], axis=1)
        row = jnp.pad(gain.reshape((n, 1, own_rows)), ((0, 0), (0, 0), (0, both.shape[1] - own_rows)))
        return jnp.concatenate([both.reshape((n, own_rows, -1)), row], axis=1)

    owned_first, owned_second = scatter_pair(
        n,
        grads_with_gain(grad_query, grad_key, grad_gain_one),
        grads_with_gain(grad_value, grad_output, grad_gain_two),
    )
    return (
        layer_output,
        grad_tokens,
        owned_first[own_rows, :own_rows],
        owned_first[:own_rows, :q_cols],
        owned_first[:own_rows, q_cols:],
        owned_second[:own_rows, :kv_cols],
        owned_second[:own_rows, kv_cols:],
        owned_second[own_rows, :own_rows],
        owned_gate,
        owned_up,
        owned_down,
    )


def solution(mesh):
    n = mesh.shape["shard"]
    tokens = P(("shard", "rep"), None)
    matrix = P("shard", None)
    vector = P("shard")

    def layer(*args):
        return per_device(n, *args)

    return jax.shard_map(
        layer,
        mesh=mesh,
        in_specs=(tokens, tokens, vector, matrix, matrix, matrix, matrix, vector)
        + (matrix,) * 3,
        out_specs=(tokens, tokens, vector, matrix, matrix, matrix, matrix, vector)
        + (matrix,) * 3,
        check_vma=False,
    )
```

time: 725 us -> 337 us (0.46)
  blocking collectives: 502 us -> 10.3 us
  waiting for transfers between devices: 2.16 us -> 81.5 us
  other arithmetic: 21.7 us -> 48.2 us
  between operations: 17.7 us -> 1.96 us
  local copies, waits for them, and re-layouts: 67.3 us -> 80 us
    unnamed x3 -> x0, blocking collectives: 326 us -> none
    all_gather x4 -> x0, blocking collectives: 172 us -> none  [the longest x1 45 us: per_device(): lax.all_gather(value_weight, 'shard', axis=0, tiled=True)]
    all_to_all x0 -> x11, waiting for transfers between devices: none -> 80.5 us  [the longest x6 44.8 us: scatter_pair(): lax.all_to_all(sent, 'shard', 0, 0, tiled=True, axis_index_groups=groups_...]
    unnamed x158 -> x134, local copies, waits for them, and re-layouts: 67.3 us -> 13 us
    all_to_all x0 -> x11, starting transfers between devices: none -> 51 us  [the longest x5 26.4 us: gather_half(): lax.all_to_all(sent, 'shard', 0, 0, tiled=True, axis_index_groups=groups_...]
    unnamed x16 -> x0, starting transfers between devices: 47.7 us -> none
    reshape x0 -> x15, local copies, waits for them, and re-layouts: none -> 22.4 us  [the longest x3 5.33 us: scatter_pair(): sent = held.reshape((left, size, rows, cols)).swapaxes(0, 1)]
    select_n x0 -> x5, local copies, waits for them, and re-layouts: none -> 14 us  [the longest x3 8.05 us: scatter_pair(): send = jnp.where(core == 0, second, first)]
  transfers between devices with their start and end apart: 21 -> 20, of which waited for: 0 -> 12; matrix products, arithmetic and copies ran while one was open for 51% -> 26% of each run, Pallas kernels for 0% -> 0%
where the time goes in v1:
time: 337 us; the launch traced here: 332 us
  waiting for transfers between devices  81.5 us (24%)
  local copies, waits for them, and re-layouts  80 us (24%)
  matrix products  57.7 us (17%)
  starting transfers between devices  52.3 us (16%)
  other arithmetic  48.2 us (14%)
  blocking collectives  10.3 us (3%)
    all_to_all x6, waiting for transfers between devices, scatter_pair(): lax.all_to_all(sent, 'shard', 0, 0, tiled=True, axis_index_groups=groups_...  44.8 us
    all_to_all x5, waiting for transfers between devices, gather_half(): lax.all_to_all(sent, 'shard', 0, 0, tiled=True, axis_index_groups=groups_...  35.7 us
    all_to_all x5, starting transfers between devices, gather_half(): lax.all_to_all(sent, 'shard', 0, 0, tiled=True, axis_index_groups=groups_...  26.4 us
    all_to_all x6, starting transfers between devices, scatter_pair(): lax.all_to_all(sent, 'shard', 0, 0, tiled=True, axis_index_groups=groups_...  24.7 us
    dot_general x7, matrix products, contract_rows(): lax.dot_general(former, latter, (((0,), (0,)), ((), ())), preferred_eleme...  13.2 us
    unnamed x134, local copies, waits for them, and re-layouts  13 us
    convert_element_type x1, other arithmetic, per_device(): grad_scores_low = grad_scores.astype(jnp.bfloat16)  11.2 us
    dot_general x7, matrix products, contract_cols(): lax.dot_general(former, latter, (((1,), (1,)), ((), ())), preferred_eleme...  10.4 us
  transfers between devices with their start and end apart: 20, of which 12 were waited for; matrix products, arithmetic and copies ran while one was open for 26% of the time, Pallas kernels for 0%

profile of v1, /device:TPU:0, one launch (start us, length us, event | category | flops | bytes accessed | tf_op | source)
XLA Modules:
  0.0 331.9 jit_solution(729263188405028338)
XLA Ops:
  2.2 6.3 %all-to-all-start.4 = ((bf16[4,1,48,576]{3,2,1,0:T(8,128)(2,1)}), bf16[4,1,48,576]{3,2,1,0:T(8,128)(2,1)S(1)}, u32[]{:S(2)}, u32[]{:S(2)}) async-start(bf16[4,1,48,576]{3,2,1,0:T(8,128)(2,1)} %broadcast_in_dim.36), calls=%async_computation.4 | async-start | bytes 491520 | tf_op jit(solution)/shard_map/all_to_all | solution.py:88
  10.8 6.3 %all-to-all-done.4 = bf16[4,1,48,576]{3,2,1,0:T(8,128)(2,1)S(1)} async-done(((bf16[4,1,48,576]{3,2,1,0:T(8,128)(2,1)}), bf16[4,1,48,576]{3,2,1,0:T(8,128)(2,1)S(1)}, u32[]{:S(2)}, u32[]{:S(2)}) %all-to-all-start.4) | async-done | bytes 221216 | tf_op jit(solution)/shard_map/all_to_all | solution.py:88
  17.1 10.3 %all_to_all.60 = bf16[4,1,37,768]{3,2,1,0:T(8,128)(2,1)S(1)} all-to-all(bf16[4,1,37,768]{3,2,1,0:T(8,128)(2,1)S(1)} %broadcast_in_dim.26), channel_id=1, replica_groups={{0,8,16,24},{2,10,18,26},{4,12,20,28},{6,14,22,30},{1,9,17,25},{3,11,19..., dimensions={0} | all-to-all | bytes 454656 | tf_op jit(solution)/shard_map/all_to_all | solution.py:88
  28.5 3.7 %all-to-all-start.5 = ((bf16[4,4,48,576]{3,2,1,0:T(8,128)(2,1)}), bf16[4,4,48,576]{3,2,1,0:T(8,128)(2,1)S(1)}, u32[]{:S(2)}, u32[]{:S(2)}) async-start(bf16[4,4,48,576]{3,2,1,0:T(8,128)(2,1)} %broadcast_in_dim.38), calls=%async_computation.5 | async-start | bytes 1966080 | tf_op jit(solution)/shard_map/all_to_all | solution.py:88
  32.3 10.0 %all-to-all-done.5 = bf16[4,4,48,576]{3,2,1,0:T(8,128)(2,1)S(1)} async-done(((bf16[4,4,48,576]{3,2,1,0:T(8,128)(2,1)}), bf16[4,4,48,576]{3,2,1,0:T(8,128)(2,1)S(1)}, u32[]{:S(2)}, u32[]{:S(2)}) %all-to-all-start.5) | async-done | bytes 884768 | tf_op jit(solution)/shard_map/all_to_all | solution.py:88
  43.5 4.2 %all-to-all-start.1 = ((bf16[4,4,37,768]{3,1,2,0:T(4,128)(2,1)}), bf16[4,4,37,768]{3,1,2,0:T(4,128)(2,1)}, u32[]{:S(2)}, u32[]{:S(2)}) async-start(bf16[4,4,37,768]{3,1,2,0:T(4,128)(2,1)} %broadcast_in_dim.30), calls=%async_computation.1 | async-start | bytes 1818624 | tf_op jit(solution)/shard_map/all_to_all | solution.py:88
  48.0 9.0 %all-to-all-done.1 = bf16[4,4,37,768]{3,1,2,0:T(4,128)(2,1)} async-done(((bf16[4,4,37,768]{3,1,2,0:T(4,128)(2,1)}), bf16[4,4,37,768]{3,1,2,0:T(4,128)(2,1)}, u32[]{:S(2)}, u32[]{:S(2)}) %all-to-all-start.1) | async-done | bytes 909344 | tf_op jit(solution)/shard_map/all_to_all | solution.py:88
  57.8 7.4 %all-to-all-start.2 = ((bf16[4,1,36,1536]{3,2,1,0:T(8,128)(2,1)}), bf16[4,1,36,1536]{3,2,1,0:T(8,128)(2,1)}, u32[]{:S(2)}, u32[]{:S(2)}) async-start(bf16[4,1,36,1536]{3,2,1,0:T(8,128)(2,1)} %broadcast_in_dim.33), calls=%async_computation.2 | async-start | bytes 983040 | tf_op jit(solution)/shard_map/all_to_all | solution.py:88
  69.0 9.3 %all-to-all-done.2 = bf16[4,1,36,1536]{3,2,1,0:T(8,128)(2,1)} async-done(((bf16[4,1,36,1536]{3,2,1,0:T(8,128)(2,1)}), bf16[4,1,36,1536]{3,2,1,0:T(8,128)(2,1)}, u32[]{:S(2)}, u32[]{:S(2)}) %all-to-all-start.2) | async-done | bytes 442400 | tf_op jit(solution)/shard_map/all_to_all | solution.py:88
  81.3 4.7 %all-to-all-start.3 = ((bf16[4,4,36,1536]{3,1,2,0:T(4,128)(2,1)}), bf16[4,4,36,1536]{3,1,2,0:T(4,128)(2,1)}, u32[]{:S(2)}, u32[]{:S(2)}) async-start(bf16[4,4,36,1536]{3,1,2,0:T(4,128)(2,1)} %broadcast_in_dim.35), calls=%async_computation.3 | async-start | bytes 3538944 | tf_op jit(solution)/shard_map/all_to_all | solution.py:88
  100.2 3.6 %copy-done = f32[3,512,512,3]{2,1,3,0:T(8,128)} copy-done((f32[3,512,512,3]{2,1,3,0:T(8,128)}, f32[3,512,512,3]{2,1,3,0:T(8,128)S(1)}, u32[]{:S(2)}) %copy-start) | copy-done | bytes 9437208
  106.8 4.1 %copy.143 = bf16[4,4,36,1536]{3,1,0,2:T(4,128)(2,1)} copy(bf16[4,4,36,1536]{3,0,2,1:T(4,128)(2,1)} %bitcast.18) | data formatting | bytes 3538944 | tf_op jit(solution)/shard_map/transpose | solution.py:95
  110.9 4.0 %reshape.291 = bf16[16,36,1536]{2,0,1:T(8,128)(2,1)} reshape(bf16[4,4,36,1536]{3,1,0,2:T(4,128)(2,1)} %copy.143) | data formatting | bytes 3538944 | tf_op jit(solution)/shard_map/reshape | solution.py:95
  119.7 6.1 %convolution_convert_fusion.6 = bf16[3,64,3,512]{3,1,2,0:T(8,128)(2,1)S(1)} fusion(bf16[512,3,64,1]{0,2,3,1:T(8,128)(2,1)S(1)} %bitcast.199, f32[3,512,512,3]{2,1,3,0:T(8,128)} %copy-done, f32[3,3,512]{2,1,0:T(4,128)S(1)} %log_add_fusion, pred[512,512]{0,1:T(8,128)(4,1)S(1)} %iota_compare_fusion.1), kind=kOutput, calls=%fused_computation.47 | convolution fusion | flops 311721984 | bytes 10504192 | tf_op jit(solution)/shard_map/gjqk,kgd->qgjd/dot_general | solution.py:199
  132.8 3.5 %reshape.292 = bf16[576,1536]{1,0:T(8,128)(2,1)} reshape(bf16[16,36,1536]{2,1,0:T(8,128)(2,1)} %copy.144) | data formatting | bytes 3538944 | tf_op jit(solution)/shard_map/reshape | solution.py:167
  136.3 3.7 %copy.145 = bf16[16,36,1536]{2,1,0:T(8,128)(2,1)} copy(bf16[16,36,1536]{2,0,1:T(8,128)(2,1)} %get-tuple-element.21) | data formatting | bytes 3538944 | tf_op jit(solution)/shard_map/jit(_where)/select_n | solution.py:102
  140.0 3.5 %reshape.293 = bf16[576,1536]{1,0:T(8,128)(2,1)} reshape(bf16[16,36,1536]{2,1,0:T(8,128)(2,1)} %copy.145) | data formatting | bytes 3538944 | tf_op jit(solution)/shard_map/reshape | solution.py:168
  146.9 4.0 %multiply_convert_fusion.1 = (bf16[512,1536]{1,0:T(8,128)(2,1)S(1)}, bf16[512,1536]{1,0:T(8,128)(2,1)}, bf16[512,1536]{1,0:T(8,128)(2,1)S(1)}) fusion(f32[512,1536]{1,0:T(8,128)S(1)} %copy-done.63, f32[512,1536]{1,0:T(8,128)S(1)} %fusion.52, bf16[512,576]{0,1:T(8,128)(2,1)S(1)} %copy-done.19, bf16[576,1536]{1,0:T(8,128)(2,1)S(1)} %copy-done.30), kind=kOutput, calls=%fused_computation.13 | convolution fusion | flops 918552576 | bytes 13369344 | tf_op jit(solution)/shard_map/dot_general | solution.py:205
  161.2 5.4 %fusion = (f32[3,3,512]{2,1,0:T(4,128)S(1)}, f32[3,512,512,3]{2,1,3,0:T(8,128)}) fusion(f32[3,512,512,3]{2,1,3,0:T(8,128)S(1)} %bitcast.169, f32[3,3,512]{2,1,0:T(4,128)S(1)} %log_add_fusion, pred[512,512]{0,1:T(8,128)(4,1)S(1)} %iota_compare_fusion.1, bf16[512,3,64,1]{0,2,3,1:T(8,128)(2,1)S(1)} %bitcast.200, bf16[512,3,3,64]{0,3,2,1:T(8,128)(2,1)S(1)} %bitcast.184), kind=kOutput, calls=%fused_computation.2 | convolution fusion | flops 313781760 | bytes 19959808 | tf_op jit(solution)/shard_map/qgjd,kgd->gjqk/dot_general | solution.py:238
  166.6 11.2 %fusion.2 = bf16[3,3,512,512]{2,3,1,0:T(8,128)(2,1)} fusion(f32[3,512,512,3]{2,1,3,0:T(8,128)} %get-tuple-element.52, f32[3,512,512,3]{2,1,3,0:T(8,128)} %copy-done, f32[3,3,512]{2,1,0:T(4,128)S(1)} %get-tuple-element.51, f32[3,3,512]{2,1,0:T(4,128)S(1)} %log_add_fusion, pred[512,512]{0,1:T(8,128)(4,1)S(1)} %iota_compare_fusion.1), kind=kLoop, calls=%fused_computation.4 | loop fusion | flops 14155776 | bytes 23891968 | tf_op jit(solution)/shard_map/convert_element_type | solution.py:251
  185.8 3.7 %convolution_convert_fusion = bf16[1536,576]{0,1:T(8,128)(2,1)} fusion(bf16[512,576]{0,1:T(8,128)(2,1)S(1)} %copy-done.48, bf16[512,1536]{1,0:T(8,128)(2,1)} %get-tuple-element.16), kind=kOutput, calls=%fused_computation.16 | convolution fusion | flops 906854400 | bytes 3932160 | tf_op jit(solution)/shard_map/dot_general | solution.py:15
  228.0 4.2 %all-to-all-start.10 = ((bf16[4,4,48,576]{3,2,1,0:T(8,128)(2,1)}), bf16[4,4,48,576]{3,2,1,0:T(8,128)(2,1)}, u32[]{:S(2)}, u32[]{:S(2)}) async-start(bf16[4,4,48,576]{3,2,1,0:T(8,128)(2,1)} %bitcast.177), calls=%async_computation.10 | async-start | bytes 1966080 | tf_op jit(solution)/shard_map/all_to_all | solution.py:117
  236.3 9.9 %all-to-all-done.10 = bf16[4,4,48,576]{3,2,1,0:T(8,128)(2,1)} async-done(((bf16[4,4,48,576]{3,2,1,0:T(8,128)(2,1)}), bf16[4,4,48,576]{3,2,1,0:T(8,128)(2,1)}, u32[]{:S(2)}, u32[]{:S(2)}) %all-to-all-start.10) | async-done | bytes 884768 | tf_op jit(solution)/shard_map/all_to_all | solution.py:117
  246.2 4.2 %all-to-all-start.6 = ((bf16[4,4,37,768]{3,1,2,0:T(4,128)(2,1)}), bf16[4,4,37,768]{3,1,2,0:T(4,128)(2,1)}, u32[]{:S(2)}, u32[]{:S(2)}) async-start(bf16[4,4,37,768]{3,1,2,0:T(4,128)(2,1)} %bitcast.181), calls=%async_computation.6 | async-start | bytes 1818624 | tf_op jit(solution)/shard_map/all_to_all | solution.py:117
  252.5 10.3 %all-to-all-done.6 = bf16[4,4,37,768]{3,1,2,0:T(4,128)(2,1)} async-done(((bf16[4,4,37,768]{3,1,2,0:T(4,128)(2,1)}), bf16[4,4,37,768]{3,1,2,0:T(4,128)(2,1)}, u32[]{:S(2)}, u32[]{:S(2)}) %all-to-all-start.6) | async-done | bytes 909344 | tf_op jit(solution)/shard_map/all_to_all | solution.py:117
  262.8 4.0 %all-to-all-start.11 = ((bf16[4,1,48,576]{3,2,1,0:T(8,128)(2,1)}), bf16[4,1,48,576]{3,2,1,0:T(8,128)(2,1)}, u32[]{:S(2)}, u32[]{:S(2)}) async-start(bf16[4,1,48,576]{3,2,1,0:T(8,128)(2,1)} %bitcast.192), calls=%async_computation.11 | async-start | bytes 491520 | tf_op jit(solution)/shard_map/all_to_all | solution.py:117
  274.9 3.6 %all-to-all-start.7 = ((bf16[4,1,37,768]{3,2,1,0:T(8,128)(2,1)}), bf16[4,1,37,768]{3,2,1,0:T(8,128)(2,1)S(1)}, u32[]{:S(2)}, u32[]{:S(2)}) async-start(bf16[4,1,37,768]{3,2,1,0:T(8,128)(2,1)} %copy.158), calls=%async_computation.7 | async-start | bytes 491520 | tf_op jit(solution)/shard_map/all_to_all | solution.py:117
  278.6 3.8 %add_convert_fusion = bf16[16,36,1536]{2,1,0:T(8,128)(2,1)S(1)} fusion(f32[16,36,1536]{2,1,0:T(8,128)} %reshape.311, bf16[16,36,1536]{2,0,1:T(8,128)(2,1)} %collective-permute-done.5), kind=kLoop, calls=%fused_computation.10 | loop fusion | flops 2654208 | bytes 7077888 | tf_op jit(solution)/shard_map/convert_element_type | solution.py:114
  285.9 3.7 %all-to-all-start.8 = ((bf16[4,4,36,1536]{3,1,2,0:T(4,128)(2,1)}), bf16[4,4,36,1536]{3,1,2,0:T(4,128)(2,1)S(1)}, u32[]{:S(2)}, u32[]{:S(2)}) async-start(bf16[4,4,36,1536]{3,1,2,0:T(4,128)(2,1)} %bitcast.165), calls=%async_computation.8 | async-start | bytes 3538944 | tf_op jit(solution)/shard_map/all_to_all | solution.py:117
  297.4 11.9 %all-to-all-done.8 = bf16[4,4,36,1536]{3,1,2,0:T(4,128)(2,1)S(1)} async-done(((bf16[4,4,36,1536]{3,1,2,0:T(4,128)(2,1)}), bf16[4,4,36,1536]{3,1,2,0:T(4,128)(2,1)S(1)}, u32[]{:S(2)}, u32[]{:S(2)}) %all-to-all-start.8) | async-done | bytes 1769504 | tf_op jit(solution)/shard_map/all_to_all | solution.py:117
  311.4 4.8 %all-to-all-start.9 = ((bf16[4,1,36,1536]{3,2,1,0:T(8,128)(2,1)}), bf16[4,1,36,1536]{3,2,1,0:T(8,128)(2,1)S(1)}, u32[]{:S(2)}, u32[]{:S(2)}) async-start(bf16[4,1,36,1536]{3,2,1,0:T(8,128)(2,1)} %copy.162), calls=%async_computation.9 | async-start | bytes 983040 | tf_op jit(solution)/shard_map/all_to_all | solution.py:117
  320.2 9.0 %all-to-all-done.9 = bf16[4,1,36,1536]{3,2,1,0:T(8,128)(2,1)S(1)} async-done(((bf16[4,1,36,1536]{3,2,1,0:T(8,128)(2,1)}), bf16[4,1,36,1536]{3,2,1,0:T(8,128)(2,1)S(1)}, u32[]{:S(2)}, u32[]{:S(2)}) %all-to-all-start.9) | async-done | bytes 442400 | tf_op jit(solution)/shard_map/all_to_all | solution.py:117
  (276 shorter events, 136.3 us)
Async XLA Ops:
  2.2 14.9 %all-to-all-start.4 = ((bf16[4,1,48,576]{3,2,1,0:T(8,128)(2,1)}), bf16[4,1,48,576]{3,2,1,0:T(8,128)(2,1)S(1)}, u32[]{:S(2)}, u32[]{:S(2)}) async-start(bf16[4,1,48,576]{3,2,1,0:T(8,128)(2,1)} %broadcast_in_dim.36), calls=%async_computation.4 | async-start | bytes 491520 | tf_op jit(solution)/shard_map/all_to_all | solution.py:88
  28.5 13.8 %all-to-all-start.5 = ((bf16[4,4,48,576]{3,2,1,0:T(8,128)(2,1)}), bf16[4,4,48,576]{3,2,1,0:T(8,128)(2,1)S(1)}, u32[]{:S(2)}, u32[]{:S(2)}) async-start(bf16[4,4,48,576]{3,2,1,0:T(8,128)(2,1)} %broadcast_in_dim.38), calls=%async_computation.5 | async-start | bytes 1966080 | tf_op jit(solution)/shard_map/all_to_all | solution.py:88
  32.2 15.5 %copy-start.54 = (bf16[36,1536]{1,0:T(8,128)(2,1)S(1)}, bf16[36,1536]{1,0:T(8,128)(2,1)}, u32[]{:S(2)}) copy-start(bf16[36,1536]{1,0:T(8,128)(2,1)} %param.19) | copy-start | bytes 331780
  32.2 15.5 %copy-start.55 = (bf16[36,1536]{1,0:T(8,128)(2,1)S(1)}, bf16[36,1536]{1,0:T(8,128)(2,1)}, u32[]{:S(2)}) copy-start(bf16[36,1536]{1,0:T(8,128)(2,1)} %param.20) | copy-start | bytes 331780
  43.5 13.5 %all-to-all-start.1 = ((bf16[4,4,37,768]{3,1,2,0:T(4,128)(2,1)}), bf16[4,4,37,768]{3,1,2,0:T(4,128)(2,1)}, u32[]{:S(2)}, u32[]{:S(2)}) async-start(bf16[4,4,37,768]{3,1,2,0:T(4,128)(2,1)} %broadcast_in_dim.30), calls=%async_computation.1 | async-start | bytes 1818624 | tf_op jit(solution)/shard_map/all_to_all | solution.py:88
  47.8 18.6 %copy-start.8 = (bf16[512,576]{0,1:T(8,128)(2,1)S(1)}, bf16[512,576]{0,1:T(8,128)(2,1)}, u32[]{:S(2)}) copy-start(bf16[512,576]{0,1:T(8,128)(2,1)} %param.11) | copy-start | bytes 1769476
  47.9 38.1 %collective-permute-start.2 = (bf16[16,48,576]{2,1,0:T(8,128)(2,1)S(1)}, bf16[16,48,576]{2,1,0:T(8,128)(2,1)}, u32[]{:S(2)}, u32[]{:S(2)}) collective-permute-start(bf16[16,48,576]{2,1,0:T(8,128)(2,1)S(1)} %bitcast.178), channel_id=1, source_target_pairs={{0,1},{1,0},{2,3},{3,2},{4,5},{5,4},{6,7},{7,6},{8,9},{9,8},{10,11... | collective-permute-start | bytes 2654216 | tf_op jit(solution)/shard_map/ppermute | solution.py:79
  57.8 20.5 %all-to-all-start.2 = ((bf16[4,1,36,1536]{3,2,1,0:T(8,128)(2,1)}), bf16[4,1,36,1536]{3,2,1,0:T(8,128)(2,1)}, u32[]{:S(2)}, u32[]{:S(2)}) async-start(bf16[4,1,36,1536]{3,2,1,0:T(8,128)(2,1)} %broadcast_in_dim.33), calls=%async_computation.2 | async-start | bytes 983040 | tf_op jit(solution)/shard_map/all_to_all | solution.py:88
  66.5 144.1 %copy-start.58 = (f32[512]{0:T(512)}, f32[512]{0:T(512)S(1)}, u32[]{:S(2)}) copy-start(f32[512]{0:T(512)S(1)} %add_rsqrt_fusion.1) | copy-start | bytes 6148
  68.9 22.7 %collective-permute-start = (bf16[16,37,768]{2,0,1:T(8,128)(2,1)}, bf16[16,37,768]{2,0,1:T(8,128)(2,1)}, u32[]{:S(2)}, u32[]{:S(2)}) collective-permute-start(bf16[16,37,768]{2,0,1:T(8,128)(2,1)} %copy.136), channel_id=1, source_target_pairs={{0,1},{1,0},{2,3},{3,2},{4,5},{5,4},{6,7},{7,6},{8,9},{9,8},{10,11... | collective-permute-start | bytes 2727944 | tf_op jit(solution)/shard_map/ppermute | solution.py:79
  81.3 25.6 %all-to-all-start.3 = ((bf16[4,4,36,1536]{3,1,2,0:T(4,128)(2,1)}), bf16[4,4,36,1536]{3,1,2,0:T(4,128)(2,1)}, u32[]{:S(2)}, u32[]{:S(2)}) async-start(bf16[4,4,36,1536]{3,1,2,0:T(4,128)(2,1)} %broadcast_in_dim.35), calls=%async_computation.3 | async-start | bytes 3538944 | tf_op jit(solution)/shard_map/all_to_all | solution.py:88
  94.2 116.4 %copy-start.56 = (f32[576]{0:T(1024)}, f32[576]{0:T(1024)S(1)}, u32[]{:S(2)}) copy-start(f32[576]{0:T(1024)S(1)} %reshape.309) | copy-start | bytes 6916
  114.9 12.7 %collective-permute-start.1 = (bf16[16,36,1536]{2,0,1:T(8,128)(2,1)}, bf16[16,36,1536]{2,0,1:T(8,128)(2,1)}, u32[]{:S(2)}, u32[]{:S(2)}) collective-permute-start(bf16[16,36,1536]{2,0,1:T(8,128)(2,1)} %reshape.291), channel_id=1, source_target_pairs={{0,1},{1,0},{2,3},{3,2},{4,5},{5,4},{6,7},{7,6},{8,9},{9,8},{10,11... | collective-permute-start | bytes 5308424 | tf_op jit(solution)/shard_map/ppermute | solution.py:79
  119.2 6.6 %copy-start.39 = (bf16[576,192]{1,0:T(8,128)(2,1)}, bf16[576,192]{1,0:T(8,128)(2,1)S(1)}, u32[]{:S(2)}) copy-start(bf16[576,192]{1,0:T(8,128)(2,1)S(1)} %reshape.285) | copy-start | bytes 663556
  119.7 6.2 %copy-start.50 = (bf16[512,192]{0,1:T(8,128)(2,1)}, bf16[512,192]{0,1:T(8,128)(2,1)S(1)}, u32[]{:S(2)}) copy-start(bf16[512,192]{0,1:T(8,128)(2,1)S(1)} %convolution_convert_fusion.9) | copy-start | bytes 589828
  126.6 27.4 %copy-start.6 = (f32[512,576]{0,1:T(8,128)}, f32[512,576]{0,1:T(8,128)S(1)}, u32[]{:S(2)}) copy-start(f32[512,576]{0,1:T(8,128)S(1)} %get-tuple-element.49) | copy-start | bytes 3538948
  150.9 7.1 %slice-start = ((s8[9437184]{0:T(1024)(128)(4,1)}), s8[4194304]{0:T(1024)(128)(4,1)S(1)}, s32[]{:S(2)}) async-start(s8[9437184]{0:T(1024)(128)(4,1)} %bitcast.168), calls=%async_computation.12 | async-start | bytes 8388608
  152.6 5.4 %slice-start.1 = ((s8[9437184]{0:T(1024)(128)(4,1)}), s8[4194304]{0:T(1024)(128)(4,1)S(1)}, s32[]{:S(2)}) async-start(s8[9437184]{0:T(1024)(128)(4,1)} %bitcast.168), calls=%async_computation.13 | async-start | bytes 8388608
  166.6 11.2 %copy-start.33 = (bf16[512,3,64,1]{0,2,3,1:T(8,128)(2,1)S(1)}, bf16[512,3,64,1]{0,2,3,1:T(8,128)(2,1)}, u32[]{:S(2)}) copy-start(bf16[512,3,64,1]{0,2,3,1:T(8,128)(2,1)} %copy-done.32) | copy-start | bytes 589828
  192.5 9.1 %copy-start.4 = (bf16[1536,576]{1,0:T(8,128)(2,1)}, bf16[1536,576]{1,0:T(8,128)(2,1)S(1)}, u32[]{:S(2)}) copy-start(bf16[1536,576]{1,0:T(8,128)(2,1)S(1)} %copy.163) | copy-start | bytes 5308420
  202.7 22.6 %collective-permute-start.7 = (bf16[16,48,576]{2,1,0:T(8,128)(2,1)}, bf16[16,48,576]{2,1,0:T(8,128)(2,1)}, u32[]{:S(2)}, u32[]{:S(2)}) collective-permute-start(bf16[16,48,576]{2,1,0:T(8,128)(2,1)} %select_bitcast_fusion), channel_id=1, source_target_pairs={{0,1},{1,0},{2,3},{3,2},{4,5},{5,4},{6,7},{7,6},{8,9},{9,8},{10,11... | collective-permute-start | bytes 2654216 | tf_op jit(solution)/shard_map/ppermute | solution.py:79
  214.1 18.2 %collective-permute-start.3 = (bf16[16,37,768]{2,0,1:T(8,128)(2,1)}, bf16[16,37,768]{2,0,1:T(8,128)(2,1)}, u32[]{:S(2)}, u32[]{:S(2)}) collective-permute-start(bf16[16,37,768]{2,0,1:T(8,128)(2,1)} %copy.155), channel_id=1, source_target_pairs={{0,1},{1,0},{2,3},{3,2},{4,5},{5,4},{6,7},{7,6},{8,9},{9,8},{10,11... | collective-permute-start | bytes 2727944 | tf_op jit(solution)/shard_map/ppermute | solution.py:79
  225.4 53.2 %collective-permute-start.5 = (bf16[16,36,1536]{2,0,1:T(8,128)(2,1)}, bf16[16,36,1536]{2,0,1:T(8,128)(2,1)}, u32[]{:S(2)}, u32[]{:S(2)}) collective-permute-start(bf16[16,36,1536]{2,0,1:T(8,128)(2,1)} %copy.159), channel_id=1, source_target_pairs={{0,1},{1,0},{2,3},{3,2},{4,5},{5,4},{6,7},{7,6},{8,9},{9,8},{10,11... | collective-permute-start | bytes 5308424 | tf_op jit(solution)/shard_map/ppermute | solution.py:79
  228.0 18.2 %all-to-all-start.10 = ((bf16[4,4,48,576]{3,2,1,0:T(8,128)(2,1)}), bf16[4,4,48,576]{3,2,1,0:T(8,128)(2,1)}, u32[]{:S(2)}, u32[]{:S(2)}) async-start(bf16[4,4,48,576]{3,2,1,0:T(8,128)(2,1)} %bitcast.177), calls=%async_computation.10 | async-start | bytes 1966080 | tf_op jit(solution)/shard_map/all_to_all | solution.py:117
  246.2 16.6 %all-to-all-start.6 = ((bf16[4,4,37,768]{3,1,2,0:T(4,128)(2,1)}), bf16[4,4,37,768]{3,1,2,0:T(4,128)(2,1)}, u32[]{:S(2)}, u32[]{:S(2)}) async-start(bf16[4,4,37,768]{3,1,2,0:T(4,128)(2,1)} %bitcast.181), calls=%async_computation.6 | async-start | bytes 1818624 | tf_op jit(solution)/shard_map/all_to_all | solution.py:117
  262.8 12.1 %all-to-all-start.11 = ((bf16[4,1,48,576]{3,2,1,0:T(8,128)(2,1)}), bf16[4,1,48,576]{3,2,1,0:T(8,128)(2,1)}, u32[]{:S(2)}, u32[]{:S(2)}) async-start(bf16[4,1,48,576]{3,2,1,0:T(8,128)(2,1)} %bitcast.192), calls=%async_computation.11 | async-start | bytes 491520 | tf_op jit(solution)/shard_map/all_to_all | solution.py:117
  274.9 10.3 %all-to-all-start.7 = ((bf16[4,1,37,768]{3,2,1,0:T(8,128)(2,1)}), bf16[4,1,37,768]{3,2,1,0:T(8,128)(2,1)S(1)}, u32[]{:S(2)}, u32[]{:S(2)}) async-start(bf16[4,1,37,768]{3,2,1,0:T(8,128)(2,1)} %copy.158), calls=%async_computation.7 | async-start | bytes 491520 | tf_op jit(solution)/shard_map/all_to_all | solution.py:117
  285.9 23.3 %all-to-all-start.8 = ((bf16[4,4,36,1536]{3,1,2,0:T(4,128)(2,1)}), bf16[4,4,36,1536]{3,1,2,0:T(4,128)(2,1)S(1)}, u32[]{:S(2)}, u32[]{:S(2)}) async-start(bf16[4,4,36,1536]{3,1,2,0:T(4,128)(2,1)} %bitcast.165), calls=%async_computation.8 | async-start | bytes 3538944 | tf_op jit(solution)/shard_map/all_to_all | solution.py:117
  296.7 19.5 %collective-permute-start.8 = (f32[48,576]{1,0:T(8,128)S(1)}, f32[48,576]{1,0:T(8,128)S(1)}, u32[]{:S(2)}, u32[]{:S(2)}) collective-permute-start(f32[48,576]{1,0:T(8,128)S(1)} %convert_reduce_fusion.1), channel_id=1, source_target_pairs={{0,1},{1,0},{2,3},{3,2},{4,5},{5,4},{6,7},{7,6},{8,9},{9,8},{10,11... | collective-permute-start | bytes 331784 | tf_op jit(solution)/shard_map/ppermute | solution.py:79
  296.8 20.1 %collective-permute-start.4 = (f32[37,768]{1,0:T(8,128)S(1)}, f32[37,768]{1,0:T(8,128)S(1)}, u32[]{:S(2)}, u32[]{:S(2)}) collective-permute-start(f32[37,768]{1,0:T(8,128)S(1)} %convert_reduce_fusion.2), channel_id=1, source_target_pairs={{0,1},{1,0},{2,3},{3,2},{4,5},{5,4},{6,7},{7,6},{8,9},{9,8},{10,11... | collective-permute-start | bytes 341000 | tf_op jit(solution)/shard_map/ppermute | solution.py:79
  311.4 17.8 %all-to-all-start.9 = ((bf16[4,1,36,1536]{3,2,1,0:T(8,128)(2,1)}), bf16[4,1,36,1536]{3,2,1,0:T(8,128)(2,1)S(1)}, u32[]{:S(2)}, u32[]{:S(2)}) async-start(bf16[4,1,36,1536]{3,2,1,0:T(8,128)(2,1)} %copy.162), calls=%async_computation.9 | async-start | bytes 983040 | tf_op jit(solution)/shard_map/all_to_all | solution.py:117
  329.2 1.6 collective-permute-start.6
  (55 other events, 127.9 us)
